TPU v7x, 256 devices: a whole 4x4x8 slice. The times are simulated.
256 devices in a mesh: veh: 32 (over z, x), req: 8 (over y, core).
Axes of the slice: x: 4, y: 4, z: 8, core: 2. Of those that a mesh axis runs over, the one named last changes fastest.
Arguments:
- vehicle_emb: bfloat16 [32768, 128], P(('veh', 'req')), may hold values from -40 to 40
- request_emb: bfloat16 [32768, 128], P('req'), may hold values from -8 to 8
- request_feat: bfloat16 [32768, 256], P('req'), may hold values from -6 to 6
- log_supply: float32 [32768], P('veh'), may hold values from -1.2 to 1.2
- log_demand: float32 [32768], P('req'), may hold values from -1.2 to 1.2
Outputs:
- assigned: float32 [32768, 256], P(('veh', 'req'))
All inputs are finite; a program needn't handle non-finite values.
Results may differ from a plain program's by a relative error of at most 0.0017.
Values may be sent and summed in bfloat16 or wider, within the bound.
A program may use at most 64 MiB of HBM per device.

v0:
```python
import math
import jax
import jax.numpy as jnp
from jax import lax
from jax.sharding import PartitionSpec as P


def local(vehicle_emb, request_emb, request_feat, log_supply, log_demand):
    own_rows = lax.all_gather(vehicle_emb, "req", axis=0, tiled=True)
    row_count = own_rows.shape[0]
    block_rows = min(256, row_count)
    block_count = row_count // block_rows
    vehicle_blocks = own_rows.reshape(block_count, block_rows, own_rows.shape[1])
    score_scale = 3.0 / math.sqrt(own_rows.shape[1])
    request_count = request_emb.shape[0]

    def block_scores(vehicle_block):
        return (
            lax.dot_general(
                vehicle_block,
                request_emb,
                (((1,), (1,)), ((), ())),
                preferred_element_type=jnp.float32,
            )
            * score_scale
        )

    def column_pot(shift):
        shift_blocks = shift.reshape(block_count, block_rows)

        def column_step(state_pair, element):
            running, accrued = state_pair
            vehicle_block, shift_block = element
            logits = block_scores(vehicle_block) + shift_block[:, None]
            highest = jnp.maximum(running, jnp.max(logits, axis=0))
            accrued = accrued * jnp.exp(running - highest) + jnp.sum(
                jnp.exp(logits - highest[None, :]), axis=0
            )
            return ((highest, accrued), None)

        start_pair = (
            jnp.full((request_count,), -1e30, jnp.float32),
            jnp.zeros((request_count,), jnp.float32),
        )
        (highest, accrued), unused = lax.scan(
            column_step, start_pair, (vehicle_blocks, shift_blocks)
        )
        summit = lax.pmax(highest, "veh")
        accrued = lax.psum(accrued * jnp.exp(highest - summit), "veh")
        highest = summit
        return log_demand - (highest + jnp.log(accrued))

    demand_first = column_pot(jnp.zeros((row_count,), jnp.float32))

    def row_block(vehicle_block):
        logits = block_scores(vehicle_block) + demand_first[None, :]
        highest = jnp.max(logits, axis=1)
        return (highest, jnp.sum(jnp.exp(logits - highest[:, None]), axis=1))

    highest, accrued = lax.map(row_block, vehicle_blocks)
    highest = highest.reshape(row_count)
    accrued = accrued.reshape(row_count)
    summit = lax.pmax(highest, "req")
    accrued = lax.psum(accrued * jnp.exp(highest - summit), "req")
    highest = summit
    supply_pot = log_supply - (highest + jnp.log(accrued))
    demand_second = column_pot(supply_pot)

    def assign_block(vehicle_block):
        logits = block_scores(vehicle_block) + demand_second[None, :]
        block_peak = jnp.max(logits, axis=1)
        powers = jnp.exp(logits - block_peak[:, None])
        block_mass = jnp.sum(powers, axis=1)
        weights = powers.astype(jnp.bfloat16)
        block_feat = jnp.dot(weights, request_feat, preferred_element_type=jnp.float32)
        return (block_peak, block_mass, block_feat)

    peaks, masses, features = lax.map(assign_block, vehicle_blocks)
    peaks = peaks.reshape(row_count)
    masses = masses.reshape(row_count)
    features = features.reshape(row_count, request_feat.shape[1])
    summit = lax.pmax(peaks, "req")
    factor = jnp.exp(peaks - summit)
    own_feat, own_mass = (
        lax.psum_scatter(features * factor[:, None], "req", scatter_dimension=0, tiled=True),
        lax.psum_scatter(masses * factor, "req", scatter_dimension=0, tiled=True),
    )
    result = own_feat / own_mass[:, None]
    return result


def solution(mesh):
    in_specs = (P(("veh", "req"), None), P("req", None), P("req", None), P("veh"), P("req"))
    out_specs = P(("veh", "req"), None)
    return jax.shard_map(local, mesh=mesh, in_specs=in_specs, out_specs=out_specs, check_vma=False)
```

profile of v0, /device:TPU:2, one launch (start us, length us, event | category | flops | bytes accessed | tf_op | source)
XLA Modules:
  0.0 732.8 jit_solution(6975081202595240819)
XLA Ops:
  6.5 13.6 %all_gather.3 = bf16[1024,128]{1,0:T(8,128)(2,1)S(1)} all-gather(bf16[128,128]{1,0:T(8,128)(2,1)} %param.13), channel_id=1, replica_groups=mesh['veh'=32,'req'=8] {'req'}, dimensions={0}, use_global_device_ids=true | all-gather | bytes 294912 | tf_op jit(solution)/shard_map/all_gather | solution.py:9
  20.1 26.8 %while.54 = (s32[]{:T(128)}, f32[4096]{0:T(1024)S(1)}, f32[4096]{0:T(1024)S(1)}, bf16[4,256,128]{2,1,0:T(8,128)(2,1)S(1)}, bf16[4096,128]{1,0:T(8,128)(2,1)}, /*index=5*/s32[]{:T(128)}, s32[]{:T(128)}) while((s32[]{:T(128)}, f32[4096]{0:T(1024)S(1)}, f32[4096]{0:T(1024)S(1)}, bf16[4,256,128]{2,1,0:T(8,128)(2,1)S(1)}, ...), condition=%wide.region_3.4_spmd.clone, body=%wide.region_0.3_spmd.clone.sunk | while | flops 272650240 | bytes 9715804 | solution.py:45
  20.1 3.9 fusion.61
  24.0 2.8 exponential_reduce_fusion.7
  26.8 3.9 fusion.61
  30.7 2.8 exponential_reduce_fusion.7
  33.5 3.9 fusion.61
  37.4 2.8 exponential_reduce_fusion.7
  40.2 3.9 fusion.61
  44.1 2.8 exponential_reduce_fusion.7
  46.9 140.6 %pmax.28 = f32[4096]{0:T(1024)S(1)} all-reduce(f32[4096]{0:T(1024)S(1)} %get-tuple-element.143), channel_id=1, replica_groups=mesh['veh'=32,'req'=8] {'veh'}, use_global_device_ids=true, to_apply=%region_4.5 | all-reduce | flops 4096 | bytes 32768 | tf_op jit(solution)/shard_map/pmax | solution.py:48
  187.6 139.9 %psum.21 = f32[4096]{0:T(1024)S(1)} all-reduce(f32[4096]{0:T(1024)S(1)} %exponential_multiply_fusion.1), channel_id=1, replica_groups=mesh['veh'=32,'req'=8] {'veh'}, use_global_device_ids=true, to_apply=%region_5.6 | all-reduce | flops 4096 | bytes 32768 | tf_op jit(solution)/shard_map/psum | solution.py:49
  327.6 11.3 %while.52 = (s32[]{:T(128)}, f32[4,256]{1,0:T(4,128)S(1)}, f32[4,256]{1,0:T(4,128)S(1)}, bf16[4,256,128]{2,1,0:T(8,128)(2,1)S(1)}, bf16[4096,128]{1,0:T(8,128)(2...) while((s32[]{:T(128)}, f32[4,256]{1,0:T(4,128)S(1)}, f32[4,256]{1,0:T(4,128)S(1)}, ...), condition=%wide.region_9.10_spmd, body=%wide.region_6.9_spmd.sunk | while | flops 273677824 | bytes 9526369 | solution.py:60
  330.4 2.0 fusion.53
  338.9 12.4 %pmax.29 = f32[1024]{0:T(1024)S(1)} all-reduce(f32[1024]{0:T(1024)S(1)} %bitcast.84), channel_id=1, replica_groups=mesh['veh'=32,'req'=8] {'req'}, use_global_device_ids=true, to_apply=%region_10.11 | all-reduce | flops 1024 | bytes 8192 | tf_op jit(solution)/shard_map/pmax | solution.py:63
  351.4 12.4 %psum.22 = f32[1024]{0:T(1024)S(1)} all-reduce(f32[1024]{0:T(1024)S(1)} %exponential_multiply_fusion.2), channel_id=1, replica_groups=mesh['veh'=32,'req'=8] {'req'}, use_global_device_ids=true, to_apply=%region_11.12 | all-reduce | flops 1024 | bytes 8192 | tf_op jit(solution)/shard_map/psum | solution.py:64
  363.8 27.0 %while.55 = (s32[]{:T(128)}, f32[4096]{0:T(1024)S(1)}, f32[4096]{0:T(1024)S(1)}, bf16[4,256,128]{2,1,0:T(8,128)(2,1)S(1)}, bf16[4096,128]{1,0:T(8,128)(2,1)}, /*index=5*/f32[4,256]{1,0:T(4,128)S(1)}, s32[]{:T(128)}, s32[]{:T(128)}) while((s32[]{:T(128)}, f32[4096]{0:T(1024)S(1)}, f32[4096]{0:T(1024)S(1)}, ...), condition=%wide.region_15.16_spmd.clone, body=%wide.region_12.15_spmd.clone.sunk | while | flops 273698816 | bytes 9718888 | solution.py:45
  363.9 4.0 fusion.64
  367.9 2.8 exponential_reduce_fusion.8
  370.7 3.9 fusion.64
  374.6 2.8 exponential_reduce_fusion.8
  377.4 3.9 fusion.64
  381.3 2.8 exponential_reduce_fusion.8
  384.2 3.9 fusion.64
  388.0 2.8 exponential_reduce_fusion.8
  390.9 137.7 %pmax.30 = f32[4096]{0:T(1024)S(1)} all-reduce(f32[4096]{0:T(1024)S(1)} %get-tuple-element.147), channel_id=1, replica_groups=mesh['veh'=32,'req'=8] {'veh'}, use_global_device_ids=true, to_apply=%region_16.17 | all-reduce | flops 4096 | bytes 32768 | tf_op jit(solution)/shard_map/pmax | solution.py:48
  528.5 137.7 %psum.23 = f32[4096]{0:T(1024)S(1)} all-reduce(f32[4096]{0:T(1024)S(1)} %exponential_multiply_fusion), channel_id=1, replica_groups=mesh['veh'=32,'req'=8] {'veh'}, use_global_device_ids=true, to_apply=%region_17.18 | all-reduce | flops 4096 | bytes 32768 | tf_op jit(solution)/shard_map/psum | solution.py:49
  666.3 14.6 %while.53 = (s32[]{:T(128)}, f32[4,256]{1,0:T(4,128)S(1)}, f32[4,256]{1,0:T(4,128)S(1)}, f32[4,256,256]{2,1,0:T(8,128)S(1)}, bf16[4,256,128]{2,1,0:T(8,128)(2,1)...) while((s32[]{:T(128)}, f32[4,256]{1,0:T(4,128)S(1)}, ...), condition=%wide.region_21.22_spmd, body=%wide.region_18.21_spmd.sunk | while | flops 812645888 | bytes 16081013 | solution.py:78
  677.3 2.0 fusion.57
  680.9 12.4 %pmax.31 = f32[1024]{0:T(1024)S(1)} all-reduce(f32[1024]{0:T(1024)S(1)} %bitcast.82), channel_id=1, replica_groups=mesh['veh'=32,'req'=8] {'req'}, use_global_device_ids=true, to_apply=%region_22.23 | all-reduce | flops 1024 | bytes 8192 | tf_op jit(solution)/shard_map/pmax | solution.py:82
  695.9 12.4 %all-reduce = f32[1024]{0:T(1024)S(1)} all-reduce(f32[1024]{0:T(1024)S(1)} %get-tuple-element.241), channel_id=3, replica_groups=mesh['veh'=32,'req'=8] {'req'}, use_global_device_ids=true, to_apply=%region_24.25.clone | all-reduce | flops 1024 | bytes 8192
  708.4 16.0 %reduce-scatter.2.cloned.1.call-done = f32[128,256]{1,0:T(8,128)} async-done(((f32[1024,256]{1,0:T(8,128)}), f32[128,256]{1,0:T(8,128)}) %reduce-scatter.2.cloned.1.call-update) | async-done | bytes 131088 | tf_op jit(solution)/shard_map/reduce_scatter | solution.py:85
  (97 shorter events, 25.7 us)
Async XLA Ops:
  6.5 717.8 %reduce-scatter.2.cloned.1.call-start = ((), (), s32[]{:S(2)}) async-start(), calls=%async_computation.1 | async-start | bytes 1179648 | tf_op jit(solution)/shard_map/reduce_scatter | solution.py:85
  20.1 307.4 %copy-start.1 = (f32[4096]{0:T(1024)S(1)}, f32[4096]{0:T(1024)}, u32[]{:S(2)}) copy-start(f32[4096]{0:T(1024)} %param.17) | copy-start | bytes 49156
  327.5 36.2 %copy-start.2 = (f32[1024]{0:T(1024)S(1)}, f32[1024]{0:T(1024)}, u32[]{:S(2)}) copy-start(f32[1024]{0:T(1024)} %param.16) | copy-start | bytes 12292
  363.8 302.4 %copy-start = (bf16[4096,256]{1,0:T(8,128)(2,1)S(1)}, bf16[4096,256]{1,0:T(8,128)(2,1)}, u32[]{:S(2)}) copy-start(bf16[4096,256]{1,0:T(8,128)(2,1)} %param.15) | copy-start | bytes 6291460
  666.3 28.3 %copy-start.3 = (u32[256]{0:T(256)S(1)}, u32[256]{0:T(256)}, u32[]{:S(2)}) copy-start(u32[256]{0:T(256)} %constant.71) | copy-start | bytes 3076
Sparse Core Ops, SparseCore 0:
  694.7 29.5 reduce-scatter.1
where the time goes:
time: 734 us; the launch traced here: 733 us
  blocking collectives  619 us (84%)
  matrix products  50.6 us (7%)
  other arithmetic  31.1 us (4%)
  waiting for transfers between devices  16 us (2%)
  between operations  14.2 us (2%)
    pmax x2, blocking collectives, column_pot(): summit = lax.pmax(highest, 'veh')  278 us
    psum x2, blocking collectives, column_pot(): accrued = lax.psum(accrued * jnp.exp(highest - summit), 'veh')  278 us
    dot_general x16, matrix products, block_scores(): lax.dot_general(vehicle_block, request_emb, (((1,), (1,)), ((), ())), pre...  47.3 us
    reduce_sum x8, other arithmetic, column_step(): jnp.sum(jnp.exp(logits - highest[None, :]), axis=0)  22.3 us
    reduce_scatter x1, waiting for transfers between devices, local(): lax.psum_scatter(features * factor[:, None], 'req', scatter_dimension=0,...  16 us
  transfers between devices with their start and end apart: 1, of which 1 were waited for; matrix products, arithmetic and copies ran while one was open for 0% of the time, Pallas kernels for 0%

commit v1 on v0

--- a/solution.py
+++ b/solution.py
@@ -46,7 +46,7 @@
             column_step, start_pair, (vehicle_blocks, shift_blocks)
         )
         summit = lax.pmax(highest, "veh")
-        accrued = lax.psum(accrued * jnp.exp(highest - summit), "veh")
+        accrued = jnp.sum(lax.all_gather(accrued * jnp.exp(highest - summit), "veh"), axis=0)
         highest = summit
         return log_demand - (highest + jnp.log(accrued))
 

time: 734 us -> 561 us (0.76)
  blocking collectives: 619 us -> 442 us
    psum x2 -> x0, blocking collectives: 278 us -> none  [column_pot(): accrued = lax.psum(accrued * jnp.exp(highest - summit), 'veh')]
    all_gather x0 -> x2, blocking collectives: none -> 103 us  [column_pot(): lax.all_gather(accrued * jnp.exp(highest - summit), 'veh')]
where the time goes in v1:
time: 561 us; the launch traced here: 559 us
  blocking collectives  442 us (79%)
  matrix products  53.4 us (10%)
  other arithmetic  32.4 us (6%)
  waiting for transfers between devices  15.2 us (3%)
  between operations  14.2 us (3%)
    pmax x2, blocking collectives, column_pot(): summit = lax.pmax(highest, 'veh')  275 us
    all_gather x2, blocking collectives, column_pot(): lax.all_gather(accrued * jnp.exp(highest - summit), 'veh')  103 us
    dot_general x16, matrix products, block_scores(): lax.dot_general(vehicle_block, request_emb, (((1,), (1,)), ((), ())), pre...  47.3 us
    reduce_sum x8, other arithmetic, column_step(): jnp.sum(jnp.exp(logits - highest[None, :]), axis=0)  22.3 us
    reduce_scatter x1, waiting for transfers between devices, local(): lax.psum_scatter(features * factor[:, None], 'req', scatter_dimension=0,...  15.2 us
    all_gather x1, blocking collectives, local(): own_rows = lax.all_gather(vehicle_emb, 'req', axis=0, tiled=True)  13.6 us
    pmax x1, blocking collectives, local(): summit = lax.pmax(highest, 'req')  12.4 us
    psum x1, blocking collectives, local(): accrued = lax.psum(accrued * jnp.exp(highest - summit), 'req')  12.4 us
  transfers between devices with their start and end apart: 1, of which 1 were waited for; matrix products, arithmetic and copies ran while one was open for 0% of the time, Pallas kernels for 0%

profile of v1, /device:TPU:2, one launch (start us, length us, event | category | flops | bytes accessed | tf_op | source)
XLA Modules:
  0.0 559.4 jit_solution(13984790037174441909)
XLA Ops:
  6.5 13.6 %all_gather.15 = bf16[1024,128]{1,0:T(8,128)(2,1)S(1)} all-gather(bf16[128,128]{1,0:T(8,128)(2,1)} %param.13), channel_id=1, replica_groups=mesh['veh'=32,'req'=8] {'req'}, dimensions={0}, use_global_device_ids=true | all-gather | bytes 294912 | tf_op jit(solution)/shard_map/all_gather | solution.py:9
  20.1 26.8 %while.54 = (s32[]{:T(128)}, f32[4096]{0:T(1024)S(1)}, f32[4096]{0:T(1024)S(1)}, bf16[4,256,128]{2,1,0:T(8,128)(2,1)S(1)}, bf16[4096,128]{1,0:T(8,128)(2,1)}, /*index=5*/s32[]{:T(128)}, s32[]{:T(128)}) while((s32[]{:T(128)}, f32[4096]{0:T(1024)S(1)}, f32[4096]{0:T(1024)S(1)}, bf16[4,256,128]{2,1,0:T(8,128)(2,1)S(1)}, ...), condition=%wide.region_3.4_spmd.clone, body=%wide.region_0.3_spmd.clone.sunk | while | flops 272650240 | bytes 9715804 | solution.py:45
  20.1 3.9 fusion.61
  24.0 2.8 exponential_reduce_fusion.7
  26.8 3.9 fusion.61
  30.7 2.8 exponential_reduce_fusion.7
  33.5 3.9 fusion.61
  37.4 2.8 exponential_reduce_fusion.7
  40.2 3.9 fusion.61
  44.1 2.8 exponential_reduce_fusion.7
  46.9 140.6 %pmax.28 = f32[4096]{0:T(1024)S(1)} all-reduce(f32[4096]{0:T(1024)S(1)} %get-tuple-element.143), channel_id=1, replica_groups=mesh['veh'=32,'req'=8] {'veh'}, use_global_device_ids=true, to_apply=%region_4.5 | all-reduce | flops 4096 | bytes 32768 | tf_op jit(solution)/shard_map/pmax | solution.py:48
  187.6 51.7 %all-gather = f32[131072]{0:T(1024)S(1)} all-gather(f32[4096]{0:T(1024)S(1)} %exponential_multiply_fusion.1), channel_id=2, replica_groups=mesh['veh'=32,'req'=8] {'veh'}, dimensions={0}, use_global_device_ids=true | all-gather | bytes 540672 | tf_op jit(solution)/shard_map/all_gather | solution.py:49
  239.5 11.4 %while.52 = (s32[]{:T(128)}, f32[4,256]{1,0:T(4,128)S(1)}, f32[4,256]{1,0:T(4,128)S(1)}, bf16[4,256,128]{2,1,0:T(8,128)(2,1)S(1)}, bf16[4096,128]{1,0:T(8,128)(2...) while((s32[]{:T(128)}, f32[4,256]{1,0:T(4,128)S(1)}, f32[4,256]{1,0:T(4,128)S(1)}, ...), condition=%wide.region_9.10_spmd, body=%wide.region_6.9_spmd.sunk | while | flops 273677824 | bytes 9526369 | solution.py:60
  242.4 2.0 fusion.53
  250.9 12.4 %pmax.29 = f32[1024]{0:T(1024)S(1)} all-reduce(f32[1024]{0:T(1024)S(1)} %bitcast.84), channel_id=1, replica_groups=mesh['veh'=32,'req'=8] {'req'}, use_global_device_ids=true, to_apply=%region_10.11 | all-reduce | flops 1024 | bytes 8192 | tf_op jit(solution)/shard_map/pmax | solution.py:63
  263.3 12.4 %psum.7 = f32[1024]{0:T(1024)S(1)} all-reduce(f32[1024]{0:T(1024)S(1)} %exponential_multiply_fusion.2), channel_id=1, replica_groups=mesh['veh'=32,'req'=8] {'req'}, use_global_device_ids=true, to_apply=%region_11.12 | all-reduce | flops 1024 | bytes 8192 | tf_op jit(solution)/shard_map/psum | solution.py:64
  275.8 27.0 %while.55 = (s32[]{:T(128)}, f32[4096]{0:T(1024)S(1)}, f32[4096]{0:T(1024)S(1)}, bf16[4,256,128]{2,1,0:T(8,128)(2,1)S(1)}, bf16[4096,128]{1,0:T(8,128)(2,1)}, /*index=5*/f32[4,256]{1,0:T(4,128)S(1)}, s32[]{:T(128)}, s32[]{:T(128)}) while((s32[]{:T(128)}, f32[4096]{0:T(1024)S(1)}, f32[4096]{0:T(1024)S(1)}, ...), condition=%wide.region_15.16_spmd.clone, body=%wide.region_12.15_spmd.clone.sunk | while | flops 273698816 | bytes 9718888 | solution.py:45
  275.8 4.0 fusion.64
  279.8 2.8 exponential_reduce_fusion.8
  282.7 3.9 fusion.64
  286.6 2.8 exponential_reduce_fusion.8
  289.4 3.9 fusion.64
  293.3 2.8 exponential_reduce_fusion.8
  296.1 3.9 fusion.64
  300.0 2.8 exponential_reduce_fusion.8
  302.9 134.8 %pmax.30 = f32[4096]{0:T(1024)S(1)} all-reduce(f32[4096]{0:T(1024)S(1)} %get-tuple-element.147), channel_id=1, replica_groups=mesh['veh'=32,'req'=8] {'veh'}, use_global_device_ids=true, to_apply=%region_16.17 | all-reduce | flops 4096 | bytes 32768 | tf_op jit(solution)/shard_map/pmax | solution.py:48
  437.7 51.7 %all-gather.1 = f32[131072]{0:T(1024)S(1)} all-gather(f32[4096]{0:T(1024)S(1)} %exponential_multiply_fusion), channel_id=3, replica_groups=mesh['veh'=32,'req'=8] {'veh'}, dimensions={0}, use_global_device_ids=true | all-gather | bytes 540672 | tf_op jit(solution)/shard_map/all_gather | solution.py:49
  489.6 17.4 %while.53 = (s32[]{:T(128)}, f32[4,256]{1,0:T(4,128)S(1)}, f32[4,256]{1,0:T(4,128)S(1)}, f32[4,256,256]{2,1,0:T(8,128)}, bf16[4,256,128]{2,1,0:T(8,128)(2,1)S(1)...) while((s32[]{:T(128)}, f32[4,256]{1,0:T(4,128)S(1)}, ...), condition=%wide.region_21.22_spmd, body=%wide.region_18.21_spmd.sunk | while | flops 812645888 | bytes 16081521 | solution.py:78
  507.1 12.4 %pmax.31 = f32[1024]{0:T(1024)S(1)} all-reduce(f32[1024]{0:T(1024)S(1)} %bitcast.82), channel_id=1, replica_groups=mesh['veh'=32,'req'=8] {'req'}, use_global_device_ids=true, to_apply=%region_22.23 | all-reduce | flops 1024 | bytes 8192 | tf_op jit(solution)/shard_map/pmax | solution.py:82
  519.5 2.4 bitcast_multiply_fusion
  523.2 12.4 %all-reduce = f32[1024]{0:T(1024)S(1)} all-reduce(f32[1024]{0:T(1024)S(1)} %get-tuple-element.241), channel_id=5, replica_groups=mesh['veh'=32,'req'=8] {'req'}, use_global_device_ids=true, to_apply=%region_24.25.clone | all-reduce | flops 1024 | bytes 8192
  535.7 15.2 %reduce-scatter.2.cloned.1.call-done = f32[128,256]{1,0:T(8,128)} async-done(((f32[1024,256]{1,0:T(8,128)}), f32[128,256]{1,0:T(8,128)}) %reduce-scatter.2.cloned.1.call-update) | async-done | bytes 131088 | tf_op jit(solution)/shard_map/reduce_scatter | solution.py:85
  (101 shorter events, 29.6 us)
Async XLA Ops:
  6.5 544.3 %reduce-scatter.2.cloned.1.call-start = ((), (), s32[]{:S(2)}) async-start(), calls=%async_computation.1 | async-start | bytes 1179648 | tf_op jit(solution)/shard_map/reduce_scatter | solution.py:85
  20.1 219.4 %copy-start.1 = (f32[4096]{0:T(1024)S(1)}, f32[4096]{0:T(1024)}, u32[]{:S(2)}) copy-start(f32[4096]{0:T(1024)} %param.17) | copy-start | bytes 49156
  239.5 36.3 %copy-start.2 = (f32[1024]{0:T(1024)S(1)}, f32[1024]{0:T(1024)}, u32[]{:S(2)}) copy-start(f32[1024]{0:T(1024)} %param.16) | copy-start | bytes 12292
  275.8 213.8 %copy-start = (bf16[4096,256]{1,0:T(8,128)(2,1)S(1)}, bf16[4096,256]{1,0:T(8,128)(2,1)}, u32[]{:S(2)}) copy-start(bf16[4096,256]{1,0:T(8,128)(2,1)} %param.15) | copy-start | bytes 6291460
  489.6 32.4 %copy-start.3 = (u32[256]{0:T(256)S(1)}, u32[256]{0:T(256)}, u32[]{:S(2)}) copy-start(u32[256]{0:T(256)} %constant.72) | copy-start | bytes 3076
Sparse Core Ops, SparseCore 0:
  522.1 28.7 reduce-scatter.1
